TPU v7x, 32 devices: a whole 2x2x4 slice. The times are simulated.
32 devices in a mesh: mp: 4 (over z), trow: 4 (over x, core), tcol: 2 (over y).
Axes of the slice: x: 2, y: 2, z: 4, core: 2. Of those that a mesh axis runs over, the one named last changes fastest.
Arguments:
- gram: float32 [4, 4096, 4096], P('mp', 'trow', 'tcol'), as said below
- rhs: float32 [256, 4096], P(('mp', 'tcol'), 'trow'), may hold values from -6 to 6
- guess: float32 [256, 4096], P(('mp', 'tcol'), 'trow'), may hold values from -6 to 6
Outputs:
- merged: float32 [256, 4096], P(('mp', 'tcol'), 'trow')
- residual: float32 [256, 4096], P(('mp', 'tcol'), 'trow')
Inputs may be any that keep to these rules, and one draw needn't show every extreme that they name: gram holds 4 symmetric positive definite matrices, one per model.
All inputs are finite; a program needn't handle non-finite values.
Results may differ from a plain program's by a relative error of at most 0.0003.
Values sent between devices are 32-bit elements; how exact they have to be, the bound alone decides.
A program may use at most 64 MiB of HBM per device.

v0:
```python
import jax
import jax.numpy as jnp
from jax import lax
from jax.sharding import PartitionSpec as P

ITERS = 2


def contract(block, weights):
    return lax.dot_general(
        block,
        weights,
        (((1,), (1,)), ((), ())),
        precision=lax.Precision.HIGHEST,
        preferred_element_type=jnp.float32,
    )


def shards(gram, rhs, guess):
    gram_tile = gram[0]
    block_cols = gram_tile.shape[1]

    def partial_terms(vector):
        columns = lax.all_gather(vector, ("mp", "tcol"), axis=0, tiled=True)
        gathered = lax.all_gather(columns, "trow", axis=1, tiled=True)
        block = lax.dynamic_slice_in_dim(
            gathered, lax.axis_index("tcol") * block_cols, block_cols, 1
        )
        return contract(block, gram_tile)

    def apply_total(vector):
        terms = partial_terms(vector)
        return lax.psum_scatter(terms, ("mp", "tcol"), scatter_dimension=0, tiled=True)

    def squares(values):
        return lax.psum(jnp.sum(values * values, axis=1), "trow")

    merged = guess
    residual = rhs - apply_total(guess)
    direction = residual
    norm_now = squares(residual)
    for step in range(ITERS):
        image = apply_total(direction)
        curve = lax.psum(jnp.sum(direction * image, axis=1), "trow")
        alpha = norm_now / curve
        merged = merged + alpha[:, None] * direction
        residual = residual - alpha[:, None] * image
        if step + 1 < ITERS:
            norm_next = squares(residual)
            direction = residual + (norm_next / norm_now)[:, None] * direction
            norm_now = norm_next
    return (merged, residual)


def solution(mesh):
    in_specs = (P("mp", "trow", "tcol"), P(("mp", "tcol"), "trow"), P(("mp", "tcol"), "trow"))
    out_specs = (P(("mp", "tcol"), "trow"), P(("mp", "tcol"), "trow"))
    return jax.shard_map(shards, mesh=mesh, in_specs=in_specs, out_specs=out_specs, check_vma=False)
```

profile of v0, /device:TPU:0, one launch (start us, length us, event | category | flops | bytes accessed | tf_op | source)
XLA Modules:
  0.0 493.4 jit_solution(17316141764370450165)
XLA Ops:
  7.2 0.7 all-gather.7.cloned.1.call-update
  7.9 45.1 %all-gather.7.cloned.1.call-done = f32[256,1024]{1,0:T(8,128)} async-done(((f32[32,1024]{1,0:T(8,128)}), f32[256,1024]{1,0:T(8,128)}) %all-gather.7.cloned.1.call-update) | async-done | bytes 1048592 | tf_op jit(solution)/shard_map/all_gather | solution.py:24
  53.1 34.7 %all-gather.9.cloned.1.call-done = f32[256,4096]{1,0:T(8,128)} async-done(((f32[256,1024]{1,0:T(8,128)}), f32[256,4096]{1,0:T(8,128)}) %all-gather.9.cloned.1.call-update) | async-done | bytes 4194320 | tf_op jit(solution)/shard_map/all_gather | solution.py:25
  87.8 11.1 %fusion.4 = f32[256,1024]{1,0:T(8,128)} fusion(f32[1,1024,2048]{2,1,0:T(8,128)} %param.3, f32[256,4096]{1,0:T(8,128)} %all-gather.9.cloned.1.call-done, s32[]{:T(128)S(6)} %select_n.2), kind=kOutput, calls=%fused_computation.4 | convolution fusion | flops 6442450944 | bytes 11534340 | tf_op jit(solution)/shard_map/dot_general | solution.py:10
  98.9 0.0 all-gather.11.cloned.1.call-start
  99.0 63.6 %reduce-scatter.4.cloned.1.call-done = f32[32,1024]{1,0:T(8,128)} async-done(((f32[256,1024]{1,0:T(8,128)}), f32[32,1024]{1,0:T(8,128)}) %reduce-scatter.4.cloned.1.call-update) | async-done | bytes 131088 | tf_op jit(solution)/shard_map/reduce_scatter | solution.py:33
  162.6 1.6 sub.9
  164.2 40.3 %all-gather.11.cloned.1.call-done = f32[256,1024]{1,0:T(8,128)} async-done(((f32[32,1024]{1,0:T(8,128)}), f32[256,1024]{1,0:T(8,128)}) %all-gather.11.cloned.1.call-update) | async-done | bytes 1048592 | tf_op jit(solution)/shard_map/all_gather | solution.py:24
  204.6 34.7 %all-gather.13.cloned.1.call-done = f32[256,4096]{1,0:T(8,128)} async-done(((f32[256,1024]{1,0:T(8,128)}), f32[256,4096]{1,0:T(8,128)}) %all-gather.13.cloned.1.call-update) | async-done | bytes 4194320 | tf_op jit(solution)/shard_map/all_gather | solution.py:25
  239.3 11.1 %fusion.2 = f32[256,1024]{1,0:T(8,128)} fusion(f32[1,1024,2048]{2,1,0:T(8,128)} %param.3, f32[256,4096]{1,0:T(8,128)} %all-gather.13.cloned.1.call-done, s32[]{:T(128)S(6)} %select_n.2), kind=kOutput, calls=%fused_computation.2 | convolution fusion | flops 6442450944 | bytes 11534340 | tf_op jit(solution)/shard_map/dot_general | solution.py:10
  250.4 63.6 %reduce-scatter.6.cloned.1.call-done = f32[32,1024]{1,0:T(8,128)} async-done(((f32[256,1024]{1,0:T(8,128)}), f32[32,1024]{1,0:T(8,128)}) %reduce-scatter.6.cloned.1.call-update) | async-done | bytes 131088 | tf_op jit(solution)/shard_map/reduce_scatter | solution.py:33
  314.1 1.0 multiply_reduce_fusion.2
  315.1 5.7 %all-reduce = (f32[32]{0:T(128)S(1)}, f32[32]{0:T(128)S(1)}) all-reduce(f32[32]{0:T(128)S(1)} %get-tuple-element.3, f32[32]{0:T(128)S(1)} %get-tuple-element.2), channel_id=1, replica_groups=mesh['mp'=4,'trow'=4,'tcol'=2] {'trow'}, use_global_device_ids=true, to_apply=%region_2.0 | all-reduce | flops 64 | bytes 512 | tf_op jit(solution)/shard_map/psum | solution.py:36
  320.8 1.1 multiply_reduce_fusion.1
  321.9 6.5 %psum.30 = f32[32]{0:T(128)S(1)} all-reduce(f32[32]{0:T(128)S(1)} %multiply_reduce_fusion.1), channel_id=1, replica_groups=mesh['mp'=4,'trow'=4,'tcol'=2] {'trow'}, use_global_device_ids=true, to_apply=%region_7.0 | all-reduce | flops 32 | bytes 256 | tf_op jit(solution)/shard_map/psum | solution.py:36
  328.4 1.7 multiply_add_fusion.1
  330.1 38.7 %all-gather.15.cloned.1.call-done = f32[256,1024]{1,0:T(8,128)} async-done(((f32[32,1024]{1,0:T(8,128)}), f32[256,1024]{1,0:T(8,128)}) %all-gather.15.cloned.1.call-update) | async-done | bytes 1048592 | tf_op jit(solution)/shard_map/all_gather | solution.py:24
  368.9 0.2 reduce-scatter.8.cloned.1.call-start
  369.2 34.5 %all-gather.17.cloned.1.call-done = f32[256,4096]{1,0:T(8,128)} async-done(((f32[256,1024]{1,0:T(8,128)}), f32[256,4096]{1,0:T(8,128)}) %all-gather.17.cloned.1.call-update) | async-done | bytes 4194320 | tf_op jit(solution)/shard_map/all_gather | solution.py:25
  403.7 11.1 %fusion = f32[256,1024]{1,0:T(8,128)} fusion(f32[1,1024,2048]{2,1,0:T(8,128)} %param.3, f32[256,4096]{1,0:T(8,128)} %all-gather.17.cloned.1.call-done, s32[]{:T(128)S(6)} %select_n.2), kind=kOutput, calls=%fused_computation | convolution fusion | flops 6442450944 | bytes 11534340 | tf_op jit(solution)/shard_map/dot_general | solution.py:10
  414.8 63.7 %reduce-scatter.8.cloned.1.call-done = f32[32,1024]{1,0:T(8,128)} async-done(((f32[256,1024]{1,0:T(8,128)}), f32[32,1024]{1,0:T(8,128)}) %reduce-scatter.8.cloned.1.call-update) | async-done | bytes 131088 | tf_op jit(solution)/shard_map/reduce_scatter | solution.py:33
  478.5 1.0 multiply_reduce_fusion
  479.5 5.7 %psum.31 = f32[32]{0:T(128)S(1)} all-reduce(f32[32]{0:T(128)S(1)} %multiply_reduce_fusion), channel_id=1, replica_groups=mesh['mp'=4,'trow'=4,'tcol'=2] {'trow'}, use_global_device_ids=true, to_apply=%region_10.0 | all-reduce | flops 32 | bytes 256 | tf_op jit(solution)/shard_map/psum | solution.py:44
  485.2 1.7 multiply_subtract_fusion
  (28 shorter events, 0.5 us)
Async XLA Ops:
  7.2 45.8 %all-gather.7.cloned.1.call-start = ((), (), s32[]{:S(2)}) async-start(), calls=%async_computation.3 | async-start | bytes 1179648 | tf_op jit(solution)/shard_map/all_gather | solution.py:24
  7.9 79.9 %all-gather.9.cloned.1.call-start = ((), (), s32[]{:S(2)}) async-start(), calls=%async_computation.4 | async-start | bytes 5242880 | tf_op jit(solution)/shard_map/all_gather | solution.py:25
  53.0 109.6 %reduce-scatter.4.cloned.1.call-start = ((), (), s32[]{:S(2)}) async-start(), calls=%async_computation.5 | async-start | bytes 1179648 | tf_op jit(solution)/shard_map/reduce_scatter | solution.py:33
  53.1 109.5 %copy-start.4 = (f32[32,1024]{1,0:T(8,128)S(1)}, f32[32,1024]{1,0:T(8,128)}, u32[]{:S(2)}) copy-start(f32[32,1024]{1,0:T(8,128)} %param.4) | copy-start | bytes 393220
  98.9 105.6 %all-gather.11.cloned.1.call-start = ((), (), s32[]{:S(2)}) async-start(), calls=%async_computation.6 | async-start | bytes 1179648 | tf_op jit(solution)/shard_map/all_gather | solution.py:24
  164.2 75.1 %all-gather.13.cloned.1.call-start = ((), (), s32[]{:S(2)}) async-start(), calls=%async_computation.7 | async-start | bytes 5242880 | tf_op jit(solution)/shard_map/all_gather | solution.py:25
  204.6 109.5 %copy-start = (f32[32,1024]{1,0:T(8,128)S(1)}, f32[32,1024]{1,0:T(8,128)}, u32[]{:S(2)}) copy-start(f32[32,1024]{1,0:T(8,128)} %sub.9) | copy-start | bytes 393220
  204.6 109.5 %reduce-scatter.6.cloned.1.call-start = ((), (), s32[]{:S(2)}) async-start(), calls=%async_computation.8 | async-start | bytes 1179648 | tf_op jit(solution)/shard_map/reduce_scatter | solution.py:33
  250.4 118.5 %all-gather.15.cloned.1.call-start = ((), (), s32[]{:S(2)}) async-start(), calls=%async_computation.9 | async-start | bytes 1179648 | tf_op jit(solution)/shard_map/all_gather | solution.py:24
  330.1 73.6 %all-gather.17.cloned.1.call-start = ((), (), s32[]{:S(2)}) async-start(), calls=%async_computation.10 | async-start | bytes 5242880 | tf_op jit(solution)/shard_map/all_gather | solution.py:25
  368.9 109.6 %copy-start.2 = (f32[32,1024]{1,0:T(8,128)S(1)}, f32[32,1024]{1,0:T(8,128)}, u32[]{:S(2)}) copy-start(f32[32,1024]{1,0:T(8,128)} %multiply_add_fusion.1) | copy-start | bytes 393220
  368.9 116.2 %copy-start.1 = (f32[32,1024]{1,0:T(8,128)S(1)}, f32[32,1024]{1,0:T(8,128)}, u32[]{:S(2)}) copy-start(f32[32,1024]{1,0:T(8,128)} %reduce-scatter.6.cloned.1.call-done) | copy-start | bytes 393220
  368.9 116.2 %copy-start.3 = (f32[32,1024]{1,0:T(8,128)S(1)}, f32[32,1024]{1,0:T(8,128)}, u32[]{:S(2)}) copy-start(f32[32,1024]{1,0:T(8,128)} %param.5) | copy-start | bytes 393220
  368.9 109.5 %reduce-scatter.8.cloned.1.call-start = ((), (), s32[]{:S(2)}) async-start(), calls=%async_computation.11 | async-start | bytes 1179648 | tf_op jit(solution)/shard_map/reduce_scatter | solution.py:33
Sparse Core Ops, SparseCore 0:
  10.1 42.8 all-gather.6
  54.6 33.2 all-gather.8
  99.0 63.4 reduce-scatter.3
  165.4 39.1 all-gather.10
  206.0 33.2 all-gather.12
  250.5 63.5 reduce-scatter.5
  330.2 38.6 all-gather.14
  370.4 33.2 all-gather.16
  414.9 63.4 reduce-scatter.7
where the time goes:
time: 494 us; the launch traced here: 493 us
  waiting for transfers between devices  420 us (85%)
  matrix products  33.2 us (7%)
  blocking collectives  17.9 us (4%)
  between operations  13.9 us (3%)
  other arithmetic  8.12 us (2%)
    reduce_scatter x3, waiting for transfers between devices, apply_total(): lax.psum_scatter(terms, ('mp', 'tcol'), scatter_dimension=0, tiled=True)  191 us
    all_gather x3, waiting for transfers between devices, partial_terms(): columns = lax.all_gather(vector, ('mp', 'tcol'), axis=0, tiled=True)  124 us
    all_gather x3, waiting for transfers between devices, partial_terms(): gathered = lax.all_gather(columns, 'trow', axis=1, tiled=True)  104 us
    dot_general x3, matrix products, contract(): lax.dot_general(block, weights, (((1,), (1,)), ((), ())), precision=lax.P...  33.2 us
    psum x2, blocking collectives, squares(): return lax.psum(jnp.sum(values * values, axis=1), 'trow')  12.2 us
  transfers between devices with their start and end apart: 9, of which 9 were waited for; matrix products, arithmetic and copies ran while one was open for 0% of the time, Pallas kernels for 0%

commit v1 on v0

v1 whole, which is shorter than its diff:
```python
import functools

import jax
import jax.numpy as jnp
from jax import lax
from jax.experimental import pallas as pl
from jax.experimental.pallas import tpu as pltpu
from jax.sharding import PartitionSpec as P

ITERS = 2
APPS = ITERS + 1
TILE = 256
MESH = pl.DeviceIdType.MESH
NT = (((1,), (1,)), ((), ()))


def swap_bits(index, bits):
    weight = 1
    out = index
    while weight <= bits:
        if (bits // weight) % 2:
            out = out + weight - 2 * weight * ((index // weight) % 2)
        weight *= 2
    return out


def kernel(Z, T, C, gram_ref, rhs_ref, guess_ref, merged_ref, residual_ref,
           stage, g_hi, g_lo, vec, own, full, prod, from_y, summed, from_z, dots, dirn, image,
           stage_sem, g1_s, g1_r, g2_s, g2_r, g3_s, g3_r, r1_s, r1_r, r2_s, r2_r, d_s, d_r):
    H = T // C
    rows, feats = guess_ref.shape
    tiles = feats // TILE
    cols = Z * C * rows
    z, t, y = lax.axis_index("mp"), lax.axis_index("trow"), lax.axis_index("tcol")
    x, c = t // H, t % H
    diagonal = x == y

    def gram_copy(n):
        return pltpu.make_async_copy(
            gram_ref.at[0, pl.ds(n * TILE, TILE)], stage.at[n], stage_sem.at[n])

    for n in range(tiles):
        gram_copy(n).start()

    def remote(src, dst, s_sem, r_sem, mp=None, trow=None, tcol=None):
        return pltpu.make_async_remote_copy(
            src_ref=src, dst_ref=dst, send_sem=s_sem, recv_sem=r_sem,
            device_id=(z if mp is None else mp, t if trow is None else trow,
                       y if tcol is None else tcol),
            device_id_type=MESH)

    barrier = pltpu.get_barrier_semaphore()
    for d in range(1, Z):
        pl.semaphore_signal(barrier, inc=1, device_id=(swap_bits(z, d), t, y), device_id_type=MESH)
    for e in range(1, T * C):
        place = (t * C + y + e) % (T * C)
        pl.semaphore_signal(barrier, inc=1, device_id=(z, place // C, place % C), device_id_type=MESH)
    pl.semaphore_wait(barrier, Z - 1 + T * C - 1)

    sends = []

    def g1(a, d):
        return remote(own.at[a, z], own.at[a, z], g1_s.at[a, d], g1_r.at[a, d], mp=swap_bits(z, d))

    def g1_in(a, d):
        zi = swap_bits(z, d)
        return remote(own.at[a, zi], own.at[a, zi], g1_s.at[a, d], g1_r.at[a, d], mp=zi)

    def g2(a, d, xp):
        zi = swap_bits(z, d)
        return remote(own.at[a, zi], full.at[a, c, zi, y], g2_s.at[a, d, xp], g2_r.at[a, d, y],
                      trow=xp * H + c, tcol=x)

    def g2_in(a, d, yp):
        zi = swap_bits(z, d)
        return remote(own.at[a, zi], full.at[a, c, zi, yp], g2_s.at[a, d, yp], g2_r.at[a, d, yp],
                      trow=y * H + c, tcol=yp)

    def g3(a, d, yp, h):
        zi = swap_bits(z, d)
        block = full.at[a, c, zi, yp]
        return remote(block, block, g3_s.at[a, d, yp, h], g3_r.at[a, d, yp, h],
                      trow=x * H + (c + h) % H)

    def g3_in(a, d, yp, h):
        zi = swap_bits(z, d)
        far = (c + H - h) % H
        block = full.at[a, far, zi, yp]
        return remote(block, block, g3_s.at[a, d, yp, h], g3_r.at[a, d, yp, h], trow=x * H + far)

    def push_plane(a, d):
        for xp in range(C):
            away = jnp.logical_not(jnp.logical_and(diagonal, x == xp))

            @pl.when(away)
            def _():
                g2(a, d, xp).start()

    def split_block(a, half, zi, yp):
        value = full[a, half, zi, yp]
        high = value.astype(jnp.bfloat16)
        low = (value - high.astype(jnp.float32)).astype(jnp.bfloat16)
        at = pl.multiple_of((zi * C + yp) * rows, rows)
        lanes = pl.ds(pl.multiple_of(half * feats, feats), feats)
        vec[pl.ds(at, rows), lanes] = high
        vec[pl.ds(cols + at, rows), lanes] = low

    def land_plane(a, d):
        zi = swap_bits(z, d)
        for yp in range(C):
            here = jnp.logical_and(diagonal, y == yp)

            @pl.when(here)
            def _():
                full[a, c, zi, yp] = own[a, zi]

            @pl.when(jnp.logical_not(here))
            def _():
                g2_in(a, d, yp).wait_recv()

            for h in range(1, H):
                g3(a, d, yp, h).start()
            split_block(a, c, zi, yp)

    def land_core(a, d):
        zi = swap_bits(z, d)
        for yp in range(C):
            for h in range(1, H):
                g3_in(a, d, yp, h).wait_recv()
                split_block(a, (c + H - h) % H, zi, yp)

    def start_gather(a):
        for d in range(Z - 1, 0, -1):
            g1(a, d).start()
        push_plane(a, 0)

    def finish_gather(a):
        for d in range(Z + 1):
            if d + 1 < Z:
                g1_in(a, d + 1).wait_recv()
                push_plane(a, d + 1)
            if d < Z:
                land_plane(a, d)
            if d >= 1:
                land_core(a, d - 1)

    def r1(a, n, dy):
        yp = (y + dy) % C
        return remote(prod.at[a, n, yp], from_y.at[a, n, dy], r1_s.at[a, n, dy], r1_r.at[a, n, dy], tcol=yp)

    def r2(a, n, d):
        zi = swap_bits(z, d)
        return remote(summed.at[a, n, zi], from_z.at[a, n, d], r2_s.at[a, n, d], r2_r.at[a, n, d], mp=zi)

    def multiply(a):
        @pl.loop(0, tiles)
        def _(n):
            at = pl.ds(pl.multiple_of(n * TILE, TILE), TILE)
            main = lax.dot_general(vec[...], g_hi[at, :], NT, preferred_element_type=jnp.float32)
            rest = lax.dot_general(vec[0:cols, :], g_lo[at, :], NT, preferred_element_type=jnp.float32)
            total = main[0:cols] + (main[cols:2 * cols] + rest)
            for zi in range(Z):
                for yp in range(C):
                    row = (zi * C + yp) * rows
                    prod[a, n, yp, zi] = total[row:row + rows]
            for dy in range(1, C):
                r1(a, n, dy).start()

    def scatter(a):
        for n in range(tiles):
            for dy in range(1, C):
                r1(a, n, dy).wait_recv()
            total = prod[a, n, y]
            for dy in range(1, C):
                total = total + from_y[a, n, dy]
            summed[a, n] = total
            for d in range(Z - 1, 0, -1):
                r2(a, n, d).start()
        for n in range(tiles):
            part = summed[a, n, z]
            for d in range(1, Z):
                r2(a, n, d).wait_recv()
                part = part + from_z[a, n, d]
            image[:, n * TILE:(n + 1) * TILE] = part

    def dot_copy(k, e):
        return remote(dots.at[k, t], dots.at[k, t], d_s.at[k, e], d_r.at[k, e], trow=(t + e) % T)

    def dot_in(k, e):
        far = (t + T - e) % T
        return remote(dots.at[k, far], dots.at[k, far], d_s.at[k, e], d_r.at[k, e], trow=far)

    def dot_start(k, value):
        dots[k, t] = jnp.broadcast_to(jnp.sum(value, axis=1, keepdims=True), (rows, 128))
        for e in range(1, T):
            dot_copy(k, e).start()

    def dot_finish(k):
        for e in range(1, T):
            dot_in(k, e).wait_recv()
        total = dots[k, 0]
        for e in range(1, T):
            total = total + dots[k, e]
        return total[:, 0:1]

    own[0, z] = guess_ref[...]
    start_gather(0)
    for n in range(tiles):
        gram_copy(n).wait()

        @pl.loop(0, TILE // 32)
        def _(i):
            value = stage[n, pl.ds(pl.multiple_of(i * 32, 32), 32)]
            high = value.astype(jnp.bfloat16)
            at = pl.ds(pl.multiple_of(n * TILE + i * 32, 32), 32)
            g_hi[at, :] = high
            g_lo[at, :] = (value - high.astype(jnp.float32)).astype(jnp.bfloat16)

    finish_gather(0)
    multiply(0)
    scatter(0)
    residual = rhs_ref[...] - image[...]
    residual_ref[...] = residual
    own[1, z] = residual
    dirn[...] = residual
    merged_ref[...] = guess_ref[...]
    start_gather(1)
    dot_start(0, residual * residual)
    norm_now = None
    for step in range(ITERS):
        a = step + 1
        finish_gather(a)
        multiply(a)
        scatter(a)
        dot_start(2 * step + 1, dirn[...] * image[...])
        if step == 0:
            norm_now = dot_finish(0)
        alpha = norm_now / dot_finish(2 * step + 1)
        residual = residual_ref[...] - alpha * image[...]
        residual_ref[...] = residual
        if step + 1 < ITERS:
            dot_start(2 * step + 2, residual * residual)
            merged_ref[...] = merged_ref[...] + alpha * dirn[...]
            norm_next = dot_finish(2 * step + 2)
            direction = residual + (norm_next / norm_now) * dirn[...]
            dirn[...] = direction
            own[a + 1, z] = direction
            start_gather(a + 1)
            norm_now = norm_next
        else:
            merged_ref[...] = merged_ref[...] + alpha * dirn[...]

    for a in range(APPS):
        for d in range(1, Z):
            g1(a, d).wait_send()
        for d in range(Z):
            for xp in range(C):
                away = jnp.logical_not(jnp.logical_and(diagonal, x == xp))

                @pl.when(away)
                def _():
                    g2(a, d, xp).wait_send()

                for h in range(1, H):
                    g3(a, d, xp, h).wait_send()
        for n in range(tiles):
            for dy in range(1, C):
                r1(a, n, dy).wait_send()
            for d in range(1, Z):
                r2(a, n, d).wait_send()
    for k in range(2 * ITERS):
        for e in range(1, T):
            dot_copy(k, e).wait_send()


def kernel_shards(Z, T, C, gram, rhs, guess):
    H = T // C
    rows, feats = guess.shape
    tiles = feats // TILE
    cols = Z * C * rows
    f32, bf16 = jnp.float32, jnp.bfloat16
    dma = pltpu.SemaphoreType.DMA
    vmem = pl.BlockSpec(memory_space=pltpu.VMEM)
    shape = jax.ShapeDtypeStruct(guess.shape, f32)
    scratch = [
        pltpu.VMEM((tiles, TILE, H * feats), f32),
        pltpu.VMEM((feats, H * feats), bf16),
        pltpu.VMEM((feats, H * feats), bf16),
        pltpu.VMEM((2 * cols, H * feats), bf16),
        pltpu.VMEM((APPS, Z, rows, feats), f32),
        pltpu.VMEM((APPS, H, Z, C, rows, feats), f32),
        pltpu.VMEM((APPS, tiles, C, Z, rows, TILE), f32),
        pltpu.VMEM((APPS, tiles, C, Z, rows, TILE), f32),
        pltpu.VMEM((APPS, tiles, Z, rows, TILE), f32),
        pltpu.VMEM((APPS, tiles, Z, rows, TILE), f32),
        pltpu.VMEM((2 * ITERS, T, rows, 128), f32),
        pltpu.VMEM((rows, feats), f32),
        pltpu.VMEM((rows, feats), f32),
        dma((tiles,)),
        dma((APPS, Z)), dma((APPS, Z)),
        dma((APPS, Z, C)), dma((APPS, Z, C)),
        dma((APPS, Z, C, H)), dma((APPS, Z, C, H)),
        dma((APPS, tiles, C)), dma((APPS, tiles, C)),
        dma((APPS, tiles, Z)), dma((APPS, tiles, Z)),
        dma((2 * ITERS, T)), dma((2 * ITERS, T)),
    ]
    return pl.pallas_call(
        functools.partial(kernel, Z, T, C),
        out_shape=(shape, shape),
        in_specs=[pl.BlockSpec(memory_space=pl.ANY), vmem, vmem],
        out_specs=(vmem, vmem),
        scratch_shapes=scratch,
        cost_estimate=pl.CostEstimate(
            flops=APPS * 6 * cols * feats * H * feats,
            bytes_accessed=gram.size * 4,
            transcendentals=0),
        compiler_params=pltpu.CompilerParams(
            collective_id=0, has_side_effects=True, vmem_limit_bytes=56 * 1024 * 1024),
    )(gram, rhs, guess)


def general_shards(gram, rhs, guess):
    gram_tile = gram[0]
    block_cols = gram_tile.shape[1]

    def apply_total(vector):
        columns = lax.all_gather(vector, ("mp", "tcol"), axis=0, tiled=True)
        gathered = lax.all_gather(columns, "trow", axis=1, tiled=True)
        block = lax.dynamic_slice_in_dim(
            gathered, lax.axis_index("tcol") * block_cols, block_cols, 1)
        terms = lax.dot_general(block, gram_tile, NT, precision=lax.Precision.HIGHEST,
                                preferred_element_type=jnp.float32)
        return lax.psum_scatter(terms, ("mp", "tcol"), scatter_dimension=0, tiled=True)

    def squares(values):
        return lax.psum(jnp.sum(values * values, axis=1), "trow")

    merged = guess
    residual = rhs - apply_total(guess)
    direction = residual
    norm_now = squares(residual)
    for step in range(ITERS):
        image = apply_total(direction)
        curve = lax.psum(jnp.sum(direction * image, axis=1), "trow")
        alpha = norm_now / curve
        merged = merged + alpha[:, None] * direction
        residual = residual - alpha[:, None] * image
        if step + 1 < ITERS:
            norm_next = squares(residual)
            direction = residual + (norm_next / norm_now)[:, None] * direction
            norm_now = norm_next
    return (merged, residual)


def solution(mesh):
    Z, T, C = mesh.shape["mp"], mesh.shape["trow"], mesh.shape["tcol"]

    def shards(gram, rhs, guess):
        rows, feats = guess.shape
        fits = T % C == 0 and Z & (Z - 1) == 0 and rows % 16 == 0 and feats % TILE == 0
        fits = fits and Z * C * rows * feats <= 256 * 1024 and gram.shape[0] == 1
        if fits:
            return kernel_shards(Z, T, C, gram, rhs, guess)
        return general_shards(gram, rhs, guess)

    in_specs = (P("mp", "trow", "tcol"), P(("mp", "tcol"), "trow"), P(("mp", "tcol"), "trow"))
    out_specs = (P(("mp", "tcol"), "trow"), P(("mp", "tcol"), "trow"))
    return jax.shard_map(shards, mesh=mesh, in_specs=in_specs, out_specs=out_specs, check_vma=False)
```

time: 494 us -> 143 us (0.29)
  waiting for transfers between devices: 420 us -> 0 us
  Pallas kernels: 0 us -> 139 us
  matrix products: 33.2 us -> 0 us
  blocking collectives: 17.9 us -> 0 us
  between operations: 13.9 us -> 0.64 us
  other arithmetic: 8.12 us -> 0 us
    all_gather x6 -> x0, waiting for transfers between devices: 228 us -> none  [the longest x3 124 us: partial_terms(): columns = lax.all_gather(vector, ('mp', 'tcol'), axis=0, tiled=True)]
    reduce_scatter x3 -> x0, waiting for transfers between devices: 191 us -> none  [apply_total(): lax.psum_scatter(terms, ('mp', 'tcol'), scatter_dimension=0, tiled=True)]
    pallas_call x0 -> x1, Pallas kernels: none -> 139 us  [kernel_shards(): pl.pallas_call(functools.partial(kernel, Z, T, C), out_shape=(shape, shap...]
    dot_general x3 -> x0, matrix products: 33.2 us -> none  [contract(): lax.dot_general(block, weights, (((1,), (1,)), ((), ())), precision=lax.P...]
    psum x3 -> x0, blocking collectives: 17.9 us -> none  [the longest x2 12.2 us: squares(): return lax.psum(jnp.sum(values * values, axis=1), 'trow')]
  transfers between devices with their start and end apart: 9 -> 0, of which waited for: 9 -> 0; matrix products, arithmetic and copies ran while one was open for 0% -> 0% of each run, Pallas kernels for 0% -> 0%
where the time goes in v1:
time: 143 us
  Pallas kernels  139 us (97%)
  local copies, waits for them, and re-layouts  3.14 us (2%)
    pallas_call x1, Pallas kernels, kernel_shards(): pl.pallas_call(functools.partial(kernel, Z, T, C), out_shape=(shape, shap...  139 us
    unnamed x2, local copies, waits for them, and re-layouts  3.14 us

profile of v1, /device:TPU:0, one launch (start us, length us, event | category | flops | bytes accessed | tf_op | source)
XLA Modules:
  0.0 143.0 jit_solution(14237198762423953867)
XLA Ops:
  0.6 139.2 %shard_map.50 = (f32[32,1024]{1,0:T(8,128)}, f32[32,1024]{1,0:T(8,128)}) custom-call(f32[1,1024,2048]{2,1,0:T(8,128)} %gram_ref.1, f32[32,1024]{1,0:T(8,128)} %rhs_ref.1, f32[32,1024]{1,0:T(8,128)} %guess_ref.1), custom_call_target="tpu_custom_call" | custom-call | flops 9663676416 | bytes 8388608 | tf_op jit(solution)/shard_map/pallas_call | solution.py:307
  139.8 1.6 %copy.7 = f32[32,1024]{1,0:T(8,128)} copy(f32[32,1024]{1,0:T(8,128)} %get-tuple-element.4) | data formatting | bytes 262144
  141.4 1.6 %copy.8 = f32[32,1024]{1,0:T(8,128)} copy(f32[32,1024]{1,0:T(8,128)} %get-tuple-element.5) | data formatting | bytes 262144

commit v2 on v1

--- a/solution.py
+++ b/solution.py
@@ -59,34 +59,56 @@
 
     sends = []
 
-    def g1(a, d):
-        return remote(own.at[a, z], own.at[a, z], g1_s.at[a, d], g1_r.at[a, d], mp=swap_bits(z, d))
-
-    def g1_in(a, d):
-        zi = swap_bits(z, d)
-        return remote(own.at[a, zi], own.at[a, zi], g1_s.at[a, d], g1_r.at[a, d], mp=zi)
+    steps = [(0, 0)] + [(k, side) for k in range(1, Z) for side in (-1, 1)]
+
+    def block_of(step):
+        return z + step[0] * step[1]
+
+    def exists(step):
+        if step[0] == 0:
+            return True
+        return z >= step[0] if step[1] < 0 else z + step[0] < Z
+
+    def when(condition, act):
+        if condition is True:
+            act()
+        else:
+            pl.when(condition)(act)
+
+    def g1(a, zi, way):
+        block = own.at[a, zi]
+        return remote(block, block, g1_s.at[a, (way + 1) // 2, zi], g1_r.at[a, zi], mp=z + way)
+
+    def pass_on(a, step, act):
+        zi = block_of(step)
+        for way in (-1, 1):
+            if step[0] == 0 or step[1] == -way:
+                more = z > 0 if way < 0 else z < Z - 1
+                if step[0]:
+                    more = jnp.logical_and(more, exists(step))
+                when(more, lambda way=way: act(g1(a, zi, way)))
 
     def g2(a, d, xp):
-        zi = swap_bits(z, d)
-        return remote(own.at[a, zi], full.at[a, c, zi, y], g2_s.at[a, d, xp], g2_r.at[a, d, y],
+        zi = block_of(d)
+        return remote(own.at[a, zi], full.at[a, c, zi, y], g2_s.at[a, zi, xp], g2_r.at[a, zi, y],
                       trow=xp * H + c, tcol=x)
 
     def g2_in(a, d, yp):
-        zi = swap_bits(z, d)
-        return remote(own.at[a, zi], full.at[a, c, zi, yp], g2_s.at[a, d, yp], g2_r.at[a, d, yp],
+        zi = block_of(d)
+        return remote(own.at[a, zi], full.at[a, c, zi, yp], g2_s.at[a, zi, yp], g2_r.at[a, zi, yp],
                       trow=y * H + c, tcol=yp)
 
     def g3(a, d, yp, h):
-        zi = swap_bits(z, d)
+        zi = block_of(d)
         block = full.at[a, c, zi, yp]
-        return remote(block, block, g3_s.at[a, d, yp, h], g3_r.at[a, d, yp, h],
+        return remote(block, block, g3_s.at[a, zi, yp, h], g3_r.at[a, zi, yp, h],
                       trow=x * H + (c + h) % H)
 
     def g3_in(a, d, yp, h):
-        zi = swap_bits(z, d)
+        zi = block_of(d)
         far = (c + H - h) % H
         block = full.at[a, far, zi, yp]
-        return remote(block, block, g3_s.at[a, d, yp, h], g3_r.at[a, d, yp, h], trow=x * H + far)
+        return remote(block, block, g3_s.at[a, zi, yp, h], g3_r.at[a, zi, yp, h], trow=x * H + far)
 
     def push_plane(a, d):
         for xp in range(C):
@@ -106,7 +128,7 @@
         vec[pl.ds(cols + at, rows), lanes] = low
 
     def land_plane(a, d):
-        zi = swap_bits(z, d)
+        zi = block_of(d)
         for yp in range(C):
             here = jnp.logical_and(diagonal, y == yp)
 
@@ -123,26 +145,31 @@
             split_block(a, c, zi, yp)
 
     def land_core(a, d):
-        zi = swap_bits(z, d)
+        zi = block_of(d)
         for yp in range(C):
             for h in range(1, H):
                 g3_in(a, d, yp, h).wait_recv()
                 split_block(a, (c + H - h) % H, zi, yp)
 
     def start_gather(a):
-        for d in range(Z - 1, 0, -1):
-            g1(a, d).start()
-        push_plane(a, 0)
+        pass_on(a, steps[0], lambda copy: copy.start())
+        push_plane(a, steps[0])
+
+    def arrive(a, step):
+        zi = block_of(step)
+        g1(a, zi, step[1]).wait_recv()
+        pass_on(a, step, lambda copy: copy.start())
+        push_plane(a, step)
 
     def finish_gather(a):
-        for d in range(Z + 1):
-            if d + 1 < Z:
-                g1_in(a, d + 1).wait_recv()
-                push_plane(a, d + 1)
-            if d < Z:
-                land_plane(a, d)
-            if d >= 1:
-                land_core(a, d - 1)
+        count = len(steps)
+        for i in range(count + 2):
+            if 1 <= i < count:
+                when(exists(steps[i]), lambda i=i: arrive(a, steps[i]))
+            if 2 <= i + 1 <= count + 1 and 0 <= i - 1 < count:
+                when(exists(steps[i - 1]), lambda i=i: land_plane(a, steps[i - 1]))
+            if 0 <= i - 2 < count:
+                when(exists(steps[i - 2]), lambda i=i: land_core(a, steps[i - 2]))
 
     def r1(a, n, dy):
         yp = (y + dy) % C
@@ -163,13 +190,19 @@
                 for yp in range(C):
                     row = (zi * C + yp) * rows
                     prod[a, n, yp, zi] = total[row:row + rows]
-            for dy in range(1, C):
-                r1(a, n, dy).start()
+
+            @pl.when(n < 2)
+            def _():
+                for dy in range(1, C):
+                    r1(a, n, dy).start()
 
     def scatter(a):
         for n in range(tiles):
             for dy in range(1, C):
                 r1(a, n, dy).wait_recv()
+                r1(a, n, dy).wait_send()
+                if n + 2 < tiles:
+                    r1(a, n + 2, dy).start()
             total = prod[a, n, y]
             for dy in range(1, C):
                 total = total + from_y[a, n, dy]
@@ -250,22 +283,22 @@
         else:
             merged_ref[...] = merged_ref[...] + alpha * dirn[...]
 
+    def end_block(a, step):
+        pass_on(a, step, lambda copy: copy.wait_send())
+        for xp in range(C):
+            away = jnp.logical_not(jnp.logical_and(diagonal, x == xp))
+
+            @pl.when(away)
+            def _():
+                g2(a, step, xp).wait_send()
+
+            for h in range(1, H):
+                g3(a, step, xp, h).wait_send()
+
     for a in range(APPS):
-        for d in range(1, Z):
-            g1(a, d).wait_send()
-        for d in range(Z):
-            for xp in range(C):
-                away = jnp.logical_not(jnp.logical_and(diagonal, x == xp))
-
-                @pl.when(away)
-                def _():
-                    g2(a, d, xp).wait_send()
-
-                for h in range(1, H):
-                    g3(a, d, xp, h).wait_send()
+        for step in steps:
+            when(exists(step), lambda: end_block(a, step))
         for n in range(tiles):
-            for dy in range(1, C):
-                r1(a, n, dy).wait_send()
             for d in range(1, Z):
                 r2(a, n, d).wait_send()
     for k in range(2 * ITERS):
@@ -297,7 +330,7 @@
         pltpu.VMEM((rows, feats), f32),
         pltpu.VMEM((rows, feats), f32),
         dma((tiles,)),
-        dma((APPS, Z)), dma((APPS, Z)),
+        dma((APPS, 2, Z)), dma((APPS, Z)),
         dma((APPS, Z, C)), dma((APPS, Z, C)),
         dma((APPS, Z, C, H)), dma((APPS, Z, C, H)),
         dma((APPS, tiles, C)), dma((APPS, tiles, C)),

time: 143 us -> 138 us (0.965)
  Pallas kernels: 139 us -> 134 us
    pallas_call x1, Pallas kernels: 139 us -> 134 us  [kernel_shards(): pl.pallas_call(functools.partial(kernel, Z, T, C), out_shape=(shape, shap...]
where the time goes in v2:
time: 138 us
  Pallas kernels  134 us (97%)
  local copies, waits for them, and re-layouts  3.14 us (2%)
    pallas_call x1, Pallas kernels, kernel_shards(): pl.pallas_call(functools.partial(kernel, Z, T, C), out_shape=(shape, shap...  134 us
    unnamed x2, local copies, waits for them, and re-layouts  3.14 us

profile of v2, /device:TPU:0, one launch (start us, length us, event | category | flops | bytes accessed | tf_op | source)
XLA Modules:
  0.0 137.8 jit_solution(2876126392408880720)
XLA Ops:
  0.6 134.0 %shard_map.50 = (f32[32,1024]{1,0:T(8,128)}, f32[32,1024]{1,0:T(8,128)}) custom-call(f32[1,1024,2048]{2,1,0:T(8,128)} %gram_ref.1, f32[32,1024]{1,0:T(8,128)} %rhs_ref.1, f32[32,1024]{1,0:T(8,128)} %guess_ref.1), custom_call_target="tpu_custom_call" | custom-call | flops 9663676416 | bytes 8388608 | tf_op jit(solution)/shard_map/pallas_call | solution.py:340
  134.6 1.6 %copy.7 = f32[32,1024]{1,0:T(8,128)} copy(f32[32,1024]{1,0:T(8,128)} %get-tuple-element.4) | data formatting | bytes 262144
  136.2 1.6 %copy.8 = f32[32,1024]{1,0:T(8,128)} copy(f32[32,1024]{1,0:T(8,128)} %get-tuple-element.5) | data formatting | bytes 262144

commit v3 on v2

--- a/solution.py
+++ b/solution.py
@@ -9,7 +9,8 @@
 
 ITERS = 2
 APPS = ITERS + 1
-TILE = 256
+TILE = 512
+GROUPS = 2
 MESH = pl.DeviceIdType.MESH
 NT = (((1,), (1,)), ((), ()))
 
@@ -28,7 +29,7 @@
            stage, g_hi, g_lo, vec, own, full, prod, from_y, summed, from_z, dots, dirn, image,
            stage_sem, g1_s, g1_r, g2_s, g2_r, g3_s, g3_r, r1_s, r1_r, r2_s, r2_r, d_s, d_r):
     H = T // C
-    rows, feats = guess_ref.shape
+    rows, feats = guess_ref.shape[0] // GROUPS, guess_ref.shape[1]
     tiles = feats // TILE
     cols = Z * C * rows
     z, t, y = lax.axis_index("mp"), lax.axis_index("trow"), lax.axis_index("tcol")
@@ -56,8 +57,6 @@
         place = (t * C + y + e) % (T * C)
         pl.semaphore_signal(barrier, inc=1, device_id=(z, place // C, place % C), device_id_type=MESH)
     pl.semaphore_wait(barrier, Z - 1 + T * C - 1)
-
-    sends = []
 
     steps = [(0, 0)] + [(k, side) for k in range(1, Z) for side in (-1, 1)]
 
@@ -101,14 +100,14 @@
     def g3(a, d, yp, h):
         zi = block_of(d)
         block = full.at[a, c, zi, yp]
-        return remote(block, block, g3_s.at[a, zi, yp, h], g3_r.at[a, zi, yp, h],
+        return remote(block, block, g3_s.at[a, zi, yp, h - 1], g3_r.at[a, zi, yp, h - 1],
                       trow=x * H + (c + h) % H)
 
     def g3_in(a, d, yp, h):
         zi = block_of(d)
         far = (c + H - h) % H
         block = full.at[a, far, zi, yp]
-        return remote(block, block, g3_s.at[a, zi, yp, h], g3_r.at[a, zi, yp, h], trow=x * H + far)
+        return remote(block, block, g3_s.at[a, zi, yp, h - 1], g3_r.at[a, zi, yp, h - 1], trow=x * H + far)
 
     def push_plane(a, d):
         for xp in range(C):
@@ -124,8 +123,8 @@
         low = (value - high.astype(jnp.float32)).astype(jnp.bfloat16)
         at = pl.multiple_of((zi * C + yp) * rows, rows)
         lanes = pl.ds(pl.multiple_of(half * feats, feats), feats)
-        vec[pl.ds(at, rows), lanes] = high
-        vec[pl.ds(cols + at, rows), lanes] = low
+        vec[a % GROUPS, pl.ds(at, rows), lanes] = high
+        vec[a % GROUPS, pl.ds(cols + at, rows), lanes] = low
 
     def land_plane(a, d):
         zi = block_of(d)
@@ -170,10 +169,11 @@
                 when(exists(steps[i - 1]), lambda i=i: land_plane(a, steps[i - 1]))
             if 0 <= i - 2 < count:
                 when(exists(steps[i - 2]), lambda i=i: land_core(a, steps[i - 2]))
+            yield
 
     def r1(a, n, dy):
         yp = (y + dy) % C
-        return remote(prod.at[a, n, yp], from_y.at[a, n, dy], r1_s.at[a, n, dy], r1_r.at[a, n, dy], tcol=yp)
+        return remote(prod.at[a, n, yp], from_y.at[a, n, dy], r1_s.at[a, n, dy - 1], r1_r.at[a, n, dy - 1], tcol=yp)
 
     def r2(a, n, d):
         zi = swap_bits(z, d)
@@ -183,8 +183,8 @@
         @pl.loop(0, tiles)
         def _(n):
             at = pl.ds(pl.multiple_of(n * TILE, TILE), TILE)
-            main = lax.dot_general(vec[...], g_hi[at, :], NT, preferred_element_type=jnp.float32)
-            rest = lax.dot_general(vec[0:cols, :], g_lo[at, :], NT, preferred_element_type=jnp.float32)
+            main = lax.dot_general(vec[a % GROUPS], g_hi[at, :], NT, preferred_element_type=jnp.float32)
+            rest = lax.dot_general(vec[a % GROUPS, 0:cols, :], g_lo[at, :], NT, preferred_element_type=jnp.float32)
             total = main[0:cols] + (main[cols:2 * cols] + rest)
             for zi in range(Z):
                 for yp in range(C):
@@ -209,12 +209,14 @@
             summed[a, n] = total
             for d in range(Z - 1, 0, -1):
                 r2(a, n, d).start()
+            yield
         for n in range(tiles):
             part = summed[a, n, z]
             for d in range(1, Z):
                 r2(a, n, d).wait_recv()
                 part = part + from_z[a, n, d]
-            image[:, n * TILE:(n + 1) * TILE] = part
+            image[a % GROUPS, :, n * TILE:(n + 1) * TILE] = part
+            yield
 
     def dot_copy(k, e):
         return remote(dots.at[k, t], dots.at[k, t], d_s.at[k, e], d_r.at[k, e], trow=(t + e) % T)
@@ -236,8 +238,61 @@
             total = total + dots[k, e]
         return total[:, 0:1]
 
-    own[0, z] = guess_ref[...]
-    start_gather(0)
+    def band(g):
+        return slice(g * rows, (g + 1) * rows)
+
+    norms = {}
+
+    def begin_update(b):
+        a, g = b // GROUPS, b % GROUPS
+        if a == 0:
+            residual = rhs_ref[band(g)] - image[g]
+            residual_ref[band(g)] = residual
+            dirn[g] = residual
+            own[b + GROUPS, z] = residual
+            start_gather(b + GROUPS)
+            dot_start(g, residual * residual)
+            merged_ref[band(g)] = guess_ref[band(g)]
+        else:
+            dot_start((2 * a - 1) * GROUPS + g, dirn[g] * image[g])
+
+    def finish_update(b):
+        a, g = b // GROUPS, b % GROUPS
+        if a == 0:
+            return
+        if a == 1:
+            norms[g] = dot_finish(g)
+        alpha = norms[g] / dot_finish((2 * a - 1) * GROUPS + g)
+        residual = residual_ref[band(g)] - alpha * image[g]
+        residual_ref[band(g)] = residual
+        if a == ITERS:
+            merged_ref[band(g)] = merged_ref[band(g)] + alpha * dirn[g]
+            return
+        k = 2 * a * GROUPS + g
+        dot_start(k, residual * residual)
+        merged_ref[band(g)] = merged_ref[band(g)] + alpha * dirn[g]
+        yield
+        norm_next = dot_finish(k)
+        direction = residual_ref[band(g)] + (norm_next / norms[g]) * dirn[g]
+        norms[g] = norm_next
+        dirn[g] = direction
+        own[b + GROUPS, z] = direction
+        start_gather(b + GROUPS)
+        yield
+
+    def in_turns(*parts):
+        parts = list(parts)
+        while parts:
+            for part in list(parts):
+                try:
+                    next(part)
+                except StopIteration:
+                    parts.remove(part)
+
+    for g in range(GROUPS):
+        own[g, z] = guess_ref[band(g)]
+    for g in range(GROUPS):
+        start_gather(g)
     for n in range(tiles):
         gram_copy(n).wait()
 
@@ -249,39 +304,21 @@
             g_hi[at, :] = high
             g_lo[at, :] = (value - high.astype(jnp.float32)).astype(jnp.bfloat16)
 
-    finish_gather(0)
-    multiply(0)
-    scatter(0)
-    residual = rhs_ref[...] - image[...]
-    residual_ref[...] = residual
-    own[1, z] = residual
-    dirn[...] = residual
-    merged_ref[...] = guess_ref[...]
-    start_gather(1)
-    dot_start(0, residual * residual)
-    norm_now = None
-    for step in range(ITERS):
-        a = step + 1
-        finish_gather(a)
-        multiply(a)
-        scatter(a)
-        dot_start(2 * step + 1, dirn[...] * image[...])
-        if step == 0:
-            norm_now = dot_finish(0)
-        alpha = norm_now / dot_finish(2 * step + 1)
-        residual = residual_ref[...] - alpha * image[...]
-        residual_ref[...] = residual
-        if step + 1 < ITERS:
-            dot_start(2 * step + 2, residual * residual)
-            merged_ref[...] = merged_ref[...] + alpha * dirn[...]
-            norm_next = dot_finish(2 * step + 2)
-            direction = residual + (norm_next / norm_now) * dirn[...]
-            dirn[...] = direction
-            own[a + 1, z] = direction
-            start_gather(a + 1)
-            norm_now = norm_next
-        else:
-            merged_ref[...] = merged_ref[...] + alpha * dirn[...]
+    turns = APPS * GROUPS
+
+    def advance(b):
+        if b >= GROUPS:
+            yield from finish_update(b - GROUPS)
+        if b < turns:
+            yield from finish_gather(b)
+
+    for b in range(GROUPS - 1):
+        in_turns(advance(b))
+    for b in range(turns):
+        multiply(b)
+        in_turns(advance(b + GROUPS - 1), scatter(b))
+        begin_update(b)
+    in_turns(advance(turns + GROUPS - 1))
 
     def end_block(a, step):
         pass_on(a, step, lambda copy: copy.wait_send())
@@ -295,21 +332,22 @@
             for h in range(1, H):
                 g3(a, step, xp, h).wait_send()
 
-    for a in range(APPS):
+    for a in range(turns):
         for step in steps:
             when(exists(step), lambda: end_block(a, step))
         for n in range(tiles):
             for d in range(1, Z):
                 r2(a, n, d).wait_send()
-    for k in range(2 * ITERS):
+    for k in range(2 * ITERS * GROUPS):
         for e in range(1, T):
             dot_copy(k, e).wait_send()
 
 
 def kernel_shards(Z, T, C, gram, rhs, guess):
     H = T // C
-    rows, feats = guess.shape
+    rows, feats = guess.shape[0] // GROUPS, guess.shape[1]
     tiles = feats // TILE
+    turns = APPS * GROUPS
     cols = Z * C * rows
     f32, bf16 = jnp.float32, jnp.bfloat16
     dma = pltpu.SemaphoreType.DMA
@@ -319,23 +357,23 @@
         pltpu.VMEM((tiles, TILE, H * feats), f32),
         pltpu.VMEM((feats, H * feats), bf16),
         pltpu.VMEM((feats, H * feats), bf16),
-        pltpu.VMEM((2 * cols, H * feats), bf16),
-        pltpu.VMEM((APPS, Z, rows, feats), f32),
-        pltpu.VMEM((APPS, H, Z, C, rows, feats), f32),
-        pltpu.VMEM((APPS, tiles, C, Z, rows, TILE), f32),
-        pltpu.VMEM((APPS, tiles, C, Z, rows, TILE), f32),
-        pltpu.VMEM((APPS, tiles, Z, rows, TILE), f32),
-        pltpu.VMEM((APPS, tiles, Z, rows, TILE), f32),
-        pltpu.VMEM((2 * ITERS, T, rows, 128), f32),
-        pltpu.VMEM((rows, feats), f32),
-        pltpu.VMEM((rows, feats), f32),
+        pltpu.VMEM((GROUPS, 2 * cols, H * feats), bf16),
+        pltpu.VMEM((turns, Z, rows, feats), f32),
+        pltpu.VMEM((turns, H, Z, C, rows, feats), f32),
+        pltpu.VMEM((turns, tiles, C, Z, rows, TILE), f32),
+        pltpu.VMEM((turns, tiles, C, Z, rows, TILE), f32),
+        pltpu.VMEM((turns, tiles, Z, rows, TILE), f32),
+        pltpu.VMEM((turns, tiles, Z, rows, TILE), f32),
+        pltpu.VMEM((2 * ITERS * GROUPS, T, rows, 128), f32),
+        pltpu.VMEM((GROUPS, rows, feats), f32),
+        pltpu.VMEM((GROUPS, rows, feats), f32),
         dma((tiles,)),
-        dma((APPS, 2, Z)), dma((APPS, Z)),
-        dma((APPS, Z, C)), dma((APPS, Z, C)),
-        dma((APPS, Z, C, H)), dma((APPS, Z, C, H)),
-        dma((APPS, tiles, C)), dma((APPS, tiles, C)),
-        dma((APPS, tiles, Z)), dma((APPS, tiles, Z)),
-        dma((2 * ITERS, T)), dma((2 * ITERS, T)),
+        dma((turns, 2, Z)), dma((turns, Z)),
+        dma((turns, Z, C)), dma((turns, Z, C)),
+        dma((turns, Z, C, H - 1)), dma((turns, Z, C, H - 1)),
+        dma((turns, tiles, C - 1)), dma((turns, tiles, C - 1)),
+        dma((turns, tiles, Z)), dma((turns, tiles, Z)),
+        dma((2 * ITERS * GROUPS, T)), dma((2 * ITERS * GROUPS, T)),
     ]
     return pl.pallas_call(
         functools.partial(kernel, Z, T, C),
@@ -344,7 +382,7 @@
         out_specs=(vmem, vmem),
         scratch_shapes=scratch,
         cost_estimate=pl.CostEstimate(
-            flops=APPS * 6 * cols * feats * H * feats,
+            flops=turns * 6 * cols * feats * H * feats,
             bytes_accessed=gram.size * 4,
             transcendentals=0),
         compiler_params=pltpu.CompilerParams(
@@ -390,8 +428,8 @@
 
     def shards(gram, rhs, guess):
         rows, feats = guess.shape
-        fits = T % C == 0 and Z & (Z - 1) == 0 and rows % 16 == 0 and feats % TILE == 0
-        fits = fits and Z * C * rows * feats <= 256 * 1024 and gram.shape[0] == 1
+        fits = T % C == 0 and Z & (Z - 1) == 0 and rows % (16 * GROUPS) == 0 and feats % TILE == 0
+        fits = fits and T > C > 1 and Z > 1 and Z * C * rows * feats <= 256 * 1024 and gram.shape[0] == 1
         if fits:
             return kernel_shards(Z, T, C, gram, rhs, guess)
         return general_shards(gram, rhs, guess)

time: 138 us -> 159 us (1.15)
  Pallas kernels: 134 us -> 154 us
    pallas_call x1, Pallas kernels: 134 us -> 154 us  [kernel_shards(): pl.pallas_call(functools.partial(kernel, Z, T, C), out_shape=(shape, shap...]
where the time goes in v3:
time: 159 us; the launch traced here: 158 us
  Pallas kernels  154 us (97%)
  local copies, waits for them, and re-layouts  3.14 us (2%)
    pallas_call x1, Pallas kernels, kernel_shards(): pl.pallas_call(functools.partial(kernel, Z, T, C), out_shape=(shape, shap...  154 us

profile of v3, /device:TPU:0, one launch (start us, length us, event | category | flops | bytes accessed | tf_op | source)
XLA Modules:
  0.0 157.9 jit_solution(11389298983021660143)
XLA Ops:
  0.6 154.2 %shard_map.50 = (f32[32,1024]{1,0:T(8,128)}, f32[32,1024]{1,0:T(8,128)}) custom-call(f32[1,1024,2048]{2,1,0:T(8,128)} %gram_ref.1, f32[32,1024]{1,0:T(8,128)} %rhs_ref.1, f32[32,1024]{1,0:T(8,128)} %guess_ref.1), custom_call_target="tpu_custom_call" | custom-call | flops 9663676416 | bytes 8388608 | tf_op jit(solution)/shard_map/pallas_call | solution.py:378
  154.8 1.6 copy.7
  156.4 1.6 copy.8

commit v4 on v2

--- a/solution.py
+++ b/solution.py
@@ -12,6 +12,7 @@
 TILE = 256
 MESH = pl.DeviceIdType.MESH
 NT = (((1,), (1,)), ((), ()))
+NN = (((1,), (0,)), ((), ()))
 
 
 def swap_bits(index, bits):
@@ -57,8 +58,6 @@
         pl.semaphore_signal(barrier, inc=1, device_id=(z, place // C, place % C), device_id_type=MESH)
     pl.semaphore_wait(barrier, Z - 1 + T * C - 1)
 
-    sends = []
-
     steps = [(0, 0)] + [(k, side) for k in range(1, Z) for side in (-1, 1)]
 
     def block_of(step):
@@ -170,6 +169,7 @@
                 when(exists(steps[i - 1]), lambda i=i: land_plane(a, steps[i - 1]))
             if 0 <= i - 2 < count:
                 when(exists(steps[i - 2]), lambda i=i: land_core(a, steps[i - 2]))
+            yield
 
     def r1(a, n, dy):
         yp = (y + dy) % C
@@ -182,9 +182,8 @@
     def multiply(a):
         @pl.loop(0, tiles)
         def _(n):
-            at = pl.ds(pl.multiple_of(n * TILE, TILE), TILE)
-            main = lax.dot_general(vec[...], g_hi[at, :], NT, preferred_element_type=jnp.float32)
-            rest = lax.dot_general(vec[0:cols, :], g_lo[at, :], NT, preferred_element_type=jnp.float32)
+            main = lax.dot_general(vec[...], g_hi[n], NN, preferred_element_type=jnp.float32)
+            rest = lax.dot_general(vec[0:cols, :], g_lo[n], NN, preferred_element_type=jnp.float32)
             total = main[0:cols] + (main[cols:2 * cols] + rest)
             for zi in range(Z):
                 for yp in range(C):
@@ -238,18 +237,29 @@
 
     own[0, z] = guess_ref[...]
     start_gather(0)
-    for n in range(tiles):
-        gram_copy(n).wait()
-
-        @pl.loop(0, TILE // 32)
-        def _(i):
-            value = stage[n, pl.ds(pl.multiple_of(i * 32, 32), 32)]
-            high = value.astype(jnp.bfloat16)
-            at = pl.ds(pl.multiple_of(n * TILE + i * 32, 32), 32)
-            g_hi[at, :] = high
-            g_lo[at, :] = (value - high.astype(jnp.float32)).astype(jnp.bfloat16)
-
-    finish_gather(0)
+    def in_turns(*parts):
+        parts = list(parts)
+        while parts:
+            for part in list(parts):
+                try:
+                    next(part)
+                except StopIteration:
+                    parts.remove(part)
+
+    def prepare():
+        for n in range(tiles):
+            gram_copy(n).wait()
+
+            @pl.loop(0, H * feats // 256)
+            def _(i):
+                at = pl.ds(pl.multiple_of(i * 256, 256), 256)
+                value = jnp.swapaxes(stage[n, :, at], 0, 1)
+                high = value.astype(jnp.bfloat16)
+                g_hi[n, at, :] = high
+                g_lo[n, at, :] = (value - high.astype(jnp.float32)).astype(jnp.bfloat16)
+            yield
+
+    in_turns(finish_gather(0), prepare())
     multiply(0)
     scatter(0)
     residual = rhs_ref[...] - image[...]
@@ -262,7 +272,7 @@
     norm_now = None
     for step in range(ITERS):
         a = step + 1
-        finish_gather(a)
+        in_turns(finish_gather(a))
         multiply(a)
         scatter(a)
         dot_start(2 * step + 1, dirn[...] * image[...])
@@ -317,8 +327,8 @@
     shape = jax.ShapeDtypeStruct(guess.shape, f32)
     scratch = [
         pltpu.VMEM((tiles, TILE, H * feats), f32),
-        pltpu.VMEM((feats, H * feats), bf16),
-        pltpu.VMEM((feats, H * feats), bf16),
+        pltpu.VMEM((tiles, H * feats, TILE), bf16),
+        pltpu.VMEM((tiles, H * feats, TILE), bf16),
         pltpu.VMEM((2 * cols, H * feats), bf16),
         pltpu.VMEM((APPS, Z, rows, feats), f32),
         pltpu.VMEM((APPS, H, Z, C, rows, feats), f32),

time: 138 us -> 140 us (1.014)
  Pallas kernels: 134 us -> 136 us
    pallas_call x1, Pallas kernels: 134 us -> 136 us  [kernel_shards(): pl.pallas_call(functools.partial(kernel, Z, T, C), out_shape=(shape, shap...]
where the time goes in v4:
time: 140 us
  Pallas kernels  136 us (97%)
  local copies, waits for them, and re-layouts  3.14 us (2%)
    pallas_call x1, Pallas kernels, kernel_shards(): pl.pallas_call(functools.partial(kernel, Z, T, C), out_shape=(shape, shap...  136 us
    unnamed x2, local copies, waits for them, and re-layouts  3.14 us

profile of v4, /device:TPU:0, one launch (start us, length us, event | category | flops | bytes accessed | tf_op | source)
XLA Modules:
  0.0 139.8 jit_solution(6743151567994043761)
XLA Ops:
  0.6 136.0 %shard_map.50 = (f32[32,1024]{1,0:T(8,128)}, f32[32,1024]{1,0:T(8,128)}) custom-call(f32[1,1024,2048]{2,1,0:T(8,128)} %gram_ref.1, f32[32,1024]{1,0:T(8,128)} %rhs_ref.1, f32[32,1024]{1,0:T(8,128)} %guess_ref.1), custom_call_target="tpu_custom_call" | custom-call | flops 9663676416 | bytes 8388608 | tf_op jit(solution)/shard_map/pallas_call | solution.py:350
  136.6 1.6 %copy.7 = f32[32,1024]{1,0:T(8,128)} copy(f32[32,1024]{1,0:T(8,128)} %get-tuple-element.4) | data formatting | bytes 262144
  138.2 1.6 %copy.8 = f32[32,1024]{1,0:T(8,128)} copy(f32[32,1024]{1,0:T(8,128)} %get-tuple-element.5) | data formatting | bytes 262144

commit v5 on v2

--- a/solution.py
+++ b/solution.py
@@ -25,8 +25,8 @@
 
 
 def kernel(Z, T, C, gram_ref, rhs_ref, guess_ref, merged_ref, residual_ref,
-           stage, g_hi, g_lo, vec, own, full, prod, from_y, summed, from_z, dots, dirn, image,
-           stage_sem, g1_s, g1_r, g2_s, g2_r, g3_s, g3_r, r1_s, r1_r, r2_s, r2_r, d_s, d_r):
+           stage, g_hi, g_lo, vec, own, relay, full, prod, from_y, summed, from_z, dots, dirn, image,
+           stage_sem, g1_s, g1_r, g2_s, g2_r, hop_s, hop_r, on_s, g3_s, g3_r, r1_s, r1_r, r2_s, r2_r, d_s, d_r):
     H = T // C
     rows, feats = guess_ref.shape
     tiles = feats // TILE
@@ -56,8 +56,6 @@
         place = (t * C + y + e) % (T * C)
         pl.semaphore_signal(barrier, inc=1, device_id=(z, place // C, place % C), device_id_type=MESH)
     pl.semaphore_wait(barrier, Z - 1 + T * C - 1)
-
-    sends = []
 
     steps = [(0, 0)] + [(k, side) for k in range(1, Z) for side in (-1, 1)]
 
@@ -110,13 +108,23 @@
         block = full.at[a, far, zi, yp]
         return remote(block, block, g3_s.at[a, zi, yp, h], g3_r.at[a, zi, yp, h], trow=x * H + far)
 
+    def hop(a, d):
+        zi = block_of(d)
+        return remote(own.at[a, zi], relay.at[a, zi], hop_s.at[a, zi], hop_r.at[a, zi], trow=(1 - x) * H + c)
+
+    def onward(a, d):
+        zi = block_of(d)
+        return remote(relay.at[a, zi], full.at[a, c, zi, y], on_s.at[a, zi], g2_r.at[a, zi, y], tcol=1 - y)
+
     def push_plane(a, d):
-        for xp in range(C):
-            away = jnp.logical_not(jnp.logical_and(diagonal, x == xp))
-
-            @pl.when(away)
-            def _():
-                g2(a, d, xp).start()
+        @pl.when(diagonal)
+        def _():
+            g2(a, d, 1 - x).start()
+
+        @pl.when(jnp.logical_not(diagonal))
+        def _():
+            hop(a, d).start()
+            g2(a, d, x).start()
 
     def split_block(a, half, zi, yp):
         value = full[a, half, zi, yp]
@@ -129,6 +137,12 @@
 
     def land_plane(a, d):
         zi = block_of(d)
+
+        @pl.when(diagonal)
+        def _():
+            hop(a, d).wait_recv()
+            onward(a, d).start()
+
         for yp in range(C):
             here = jnp.logical_and(diagonal, y == yp)
 
@@ -285,13 +299,17 @@
 
     def end_block(a, step):
         pass_on(a, step, lambda copy: copy.wait_send())
+        @pl.when(diagonal)
+        def _():
+            g2(a, step, 1 - x).wait_send()
+            onward(a, step).wait_send()
+
+        @pl.when(jnp.logical_not(diagonal))
+        def _():
+            hop(a, step).wait_send()
+            g2(a, step, x).wait_send()
+
         for xp in range(C):
-            away = jnp.logical_not(jnp.logical_and(diagonal, x == xp))
-
-            @pl.when(away)
-            def _():
-                g2(a, step, xp).wait_send()
-
             for h in range(1, H):
                 g3(a, step, xp, h).wait_send()
 
@@ -321,6 +339,7 @@
         pltpu.VMEM((feats, H * feats), bf16),
         pltpu.VMEM((2 * cols, H * feats), bf16),
         pltpu.VMEM((APPS, Z, rows, feats), f32),
+        pltpu.VMEM((APPS, Z, rows, feats), f32),
         pltpu.VMEM((APPS, H, Z, C, rows, feats), f32),
         pltpu.VMEM((APPS, tiles, C, Z, rows, TILE), f32),
         pltpu.VMEM((APPS, tiles, C, Z, rows, TILE), f32),
@@ -332,6 +351,7 @@
         dma((tiles,)),
         dma((APPS, 2, Z)), dma((APPS, Z)),
         dma((APPS, Z, C)), dma((APPS, Z, C)),
+        dma((APPS, Z)), dma((APPS, Z)), dma((APPS, Z)),
         dma((APPS, Z, C, H)), dma((APPS, Z, C, H)),
         dma((APPS, tiles, C)), dma((APPS, tiles, C)),
         dma((APPS, tiles, Z)), dma((APPS, tiles, Z)),
@@ -390,7 +410,7 @@
 
     def shards(gram, rhs, guess):
         rows, feats = guess.shape
-        fits = T % C == 0 and Z & (Z - 1) == 0 and rows % 16 == 0 and feats % TILE == 0
+        fits = T % C == 0 and C == 2 and T == C * (T // C) and Z & (Z - 1) == 0 and rows % 16 == 0 and feats % TILE == 0
         fits = fits and Z * C * rows * feats <= 256 * 1024 and gram.shape[0] == 1
         if fits:
             return kernel_shards(Z, T, C, gram, rhs, guess)

time: 138 us -> 170 us (1.23); the launches traced: 138 us -> 168 us
  Pallas kernels: 134 us -> 164 us
    pallas_call x1, Pallas kernels: 134 us -> 164 us  [kernel_shards(): pl.pallas_call(functools.partial(kernel, Z, T, C), out_shape=(shape, shap...]
where the time goes in v5:
time: 170 us; the launch traced here: 168 us
  Pallas kernels  164 us (96%)
  local copies, waits for them, and re-layouts  3.14 us (2%)
    pallas_call x1, Pallas kernels, kernel_shards(): pl.pallas_call(functools.partial(kernel, Z, T, C), out_shape=(shape, shap...  164 us

profile of v5, /device:TPU:0, one launch (start us, length us, event | category | flops | bytes accessed | tf_op | source)
XLA Modules:
  0.0 167.6 jit_solution(9389708165164057584)
XLA Ops:
  0.6 163.8 %shard_map.50 = (f32[32,1024]{1,0:T(8,128)}, f32[32,1024]{1,0:T(8,128)}) custom-call(f32[1,1024,2048]{2,1,0:T(8,128)} %gram_ref.1, f32[32,1024]{1,0:T(8,128)} %rhs_ref.1, f32[32,1024]{1,0:T(8,128)} %guess_ref.1), custom_call_target="tpu_custom_call" | custom-call | flops 9663676416 | bytes 8388608 | tf_op jit(solution)/shard_map/pallas_call | solution.py:360
  164.5 1.6 copy.7
  166.1 1.6 copy.8

commit v6 on v2

--- a/solution.py
+++ b/solution.py
@@ -57,8 +57,6 @@
         pl.semaphore_signal(barrier, inc=1, device_id=(z, place // C, place % C), device_id_type=MESH)
     pl.semaphore_wait(barrier, Z - 1 + T * C - 1)
 
-    sends = []
-
     steps = [(0, 0)] + [(k, side) for k in range(1, Z) for side in (-1, 1)]
 
     def block_of(step):
@@ -162,14 +160,13 @@
         push_plane(a, step)
 
     def finish_gather(a):
-        count = len(steps)
-        for i in range(count + 2):
-            if 1 <= i < count:
-                when(exists(steps[i]), lambda i=i: arrive(a, steps[i]))
-            if 2 <= i + 1 <= count + 1 and 0 <= i - 1 < count:
-                when(exists(steps[i - 1]), lambda i=i: land_plane(a, steps[i - 1]))
-            if 0 <= i - 2 < count:
-                when(exists(steps[i - 2]), lambda i=i: land_core(a, steps[i - 2]))
+        for step in steps[1:]:
+            when(exists(step), lambda: arrive(a, step))
+        for i in range(len(steps) + 1):
+            if i < len(steps):
+                when(exists(steps[i]), lambda: land_plane(a, steps[i]))
+            if i >= 1:
+                when(exists(steps[i - 1]), lambda: land_core(a, steps[i - 1]))
 
     def r1(a, n, dy):
         yp = (y + dy) % C

time: 138 us -> 131 us (0.949)
  Pallas kernels: 134 us -> 127 us
    pallas_call x1, Pallas kernels: 134 us -> 127 us  [kernel_shards(): pl.pallas_call(functools.partial(kernel, Z, T, C), out_shape=(shape, shap...]
where the time goes in v6:
time: 131 us
  Pallas kernels  127 us (97%)
  local copies, waits for them, and re-layouts  3.14 us (2%)
    pallas_call x1, Pallas kernels, kernel_shards(): pl.pallas_call(functools.partial(kernel, Z, T, C), out_shape=(shape, shap...  127 us
    unnamed x2, local copies, waits for them, and re-layouts  3.14 us

profile of v6, /device:TPU:0, one launch (start us, length us, event | category | flops | bytes accessed | tf_op | source)
XLA Modules:
  0.0 130.9 jit_solution(1373324300405088458)
XLA Ops:
  0.6 127.2 %shard_map.50 = (f32[32,1024]{1,0:T(8,128)}, f32[32,1024]{1,0:T(8,128)}) custom-call(f32[1,1024,2048]{2,1,0:T(8,128)} %gram_ref.1, f32[32,1024]{1,0:T(8,128)} %rhs_ref.1, f32[32,1024]{1,0:T(8,128)} %guess_ref.1), custom_call_target="tpu_custom_call" | custom-call | flops 9663676416 | bytes 8388608 | tf_op jit(solution)/shard_map/pallas_call | solution.py:337
  127.8 1.6 %copy.7 = f32[32,1024]{1,0:T(8,128)} copy(f32[32,1024]{1,0:T(8,128)} %get-tuple-element.4) | data formatting | bytes 262144
  129.4 1.6 %copy.8 = f32[32,1024]{1,0:T(8,128)} copy(f32[32,1024]{1,0:T(8,128)} %get-tuple-element.5) | data formatting | bytes 262144
